TPU v7x, 32 devices: a whole 2x2x4 slice. The times are simulated.
32 devices in a mesh: grp: 2 (over y), chan: 4 (over z), tm: 2 (over x), lag: 2 (over core).
Axes of the slice: x: 2, y: 2, z: 4, core: 2. Of those that a mesh axis runs over, the one named last changes fastest.
Arguments:
- records: bfloat16 [4, 4, 2048, 256], P(('grp', 'tm'), 'chan'), parts along dimension 0, may hold values from -180 to 180, as said below
- dead_mask: int32 [512], P('grp'), parts along dimension 0, may hold values 0 or 1
- block_map: int32 [8], P('grp'), parts along dimension 0, may hold values from 0 to 3, each once
Outputs:
- correlations: float32 [4096, 2, 256], P(('grp', 'tm', 'lag'), None, 'chan'), parts along dimension 0
There are 2 independent parts, one for each index of `grp`. A program takes and returns all parts, laid end to end along the dimension named above; each array names one. Nothing has to cross between parts.
Inputs may be any that keep to these rules, and one draw needn't show every extreme that they name: block_map is a permutation of the block numbers. `records`: values are finite.
All inputs are finite; a program needn't handle non-finite values.
Results may differ from a plain program's by a relative error of at most 0.015.
Values may be sent and summed in bfloat16 or wider, within the bound.
A program may use at most 64 MiB of HBM per device.

v0:
```python
import math

import jax
import jax.numpy as jnp
from jax import lax
from jax.sharding import PartitionSpec as P

BAND = 16


def passed_along(shard, axis, by):
    count = lax.axis_size(axis)
    return lax.ppermute(shard, axis, [(i, (i + by) % count) for i in range(count)])


def trig_table(row_index, bin_index, samples):
    phase = row_index[:, None] * bin_index[None, :] % samples
    angle = phase.astype(jnp.float32) * (2.0 * math.pi / samples)
    return jnp.concatenate([jnp.cos(angle), -jnp.sin(angle)], axis=1).astype(jnp.bfloat16)


def band_gain(bin_index, samples):
    freq = bin_index.astype(jnp.float32)
    ramp_width = float(max(samples // 128, 1))
    lower = jnp.clip((freq - float(samples // 256)) / ramp_width, 0.0, 1.0)
    upper = jnp.clip((0.45 * samples - freq) / ramp_width, 0.0, 1.0)
    return lower * upper


def band_power(values, band_size):
    half_bins = values.shape[-1] // 2
    real_part = values[..., :half_bins]
    imag_part = values[..., half_bins:]
    power = real_part * real_part + imag_part * imag_part
    frame_total = power.shape[0]
    chan_total = power.shape[1]
    return jnp.sum(
        power.reshape(frame_total, chan_total, half_bins // band_size, band_size), axis=(0, 3)
    )


def apply_white(values, banded, bin_index, samples, band_size):
    factor = (
        jnp.repeat(1.0 / jnp.sqrt(banded + 1e-06), band_size, axis=1)
        * band_gain(bin_index, samples)[None, :]
    )
    factor = jnp.concatenate([factor, factor], axis=1)
    return (values * factor[None]).astype(jnp.bfloat16)


def cross_spectrum(own, other):
    half_bins = own.shape[-1] // 2
    own_real = own[..., :half_bins].astype(jnp.float32)
    own_imag = own[..., half_bins:].astype(jnp.float32)
    other_real = other[..., :half_bins].astype(jnp.float32)
    other_imag = other[..., half_bins:].astype(jnp.float32)
    real_sum = jnp.sum(own_real * other_real + own_imag * other_imag, axis=0)
    imag_sum = jnp.sum(own_imag * other_real - own_real * other_imag, axis=0)
    return jnp.concatenate([real_sum, imag_sum], axis=1)


def body(records, dead_mask, block_map):
    chan_total = lax.axis_size("chan")
    lag_total = lax.axis_size("lag")
    time_total = lax.axis_size("tm")
    core = lax.axis_index("lag")
    samples = records.shape[2]
    all_channels = records.shape[3]
    block_width = all_channels // chan_total
    half_bins = samples // (2 * lag_total)
    frame_count = records.shape[1] * chan_total
    bin_index = core * half_bins + jnp.arange(half_bins, dtype=jnp.int32)
    row_index = jnp.arange(samples, dtype=jnp.int32)
    forward = trig_table(row_index, bin_index, samples)
    live = records * dead_mask.astype(jnp.bfloat16)[None, None, None, :]
    split_shape = live.shape[:3] + (chan_total, block_width)
    ordered = jnp.take(live.reshape(split_shape), block_map, axis=3).reshape(live.shape)
    rounds = min(4, chan_total // 2)
    regrouped = lax.all_to_all(ordered, "chan", split_axis=3, concat_axis=1, tiled=True)
    spectra = jnp.einsum(
        "gfnc,nk->gfck", regrouped, forward, preferred_element_type=jnp.float32
    ).astype(jnp.bfloat16)
    values = spectra[0].astype(jnp.float32)
    banded = band_power(values, BAND) / float(frame_count * BAND)
    whitened = apply_white(values, banded, bin_index, samples, BAND)
    columns = []
    moving = whitened
    for offset in range(rounds):
        moving = passed_along(moving, "chan", 1)
        columns.append(cross_spectrum(whitened, moving))
    stacked = jnp.stack(columns).astype(jnp.bfloat16)
    flat = stacked.reshape(rounds * block_width, 2 * half_bins)
    lag_rows = samples // (time_total * lag_total)
    lag_index = jnp.arange(lag_rows * lax.axis_size(("tm", "lag")), dtype=jnp.int32) + samples // 2
    inverse = trig_table(lag_index, bin_index, samples)
    summed = lax.psum_scatter(
        lax.dot_general(
            inverse, flat, (((1,), (1,)), ((), ())), preferred_element_type=jnp.float32
        ),
        ("tm", "lag"),
        scatter_dimension=0,
        tiled=True,
    )
    norm = 1.0 / math.sqrt(samples // 2 * frame_count * time_total)
    return (summed * norm).reshape(lag_rows, rounds, block_width)


def solution(mesh):
    placed = (P(("grp", "tm"), "chan", None, None), P("grp"), P("grp"))
    return jax.shard_map(
        body,
        mesh=mesh,
        in_specs=placed,
        out_specs=P(("grp", "tm", "lag"), None, "chan"),
        check_vma=False,
    )
```

profile of v0, /device:TPU:1, one launch (start us, length us, event | category | flops | bytes accessed | tf_op | source)
XLA Modules:
  0.0 138.9 jit_solution(4474871248308550790)
XLA Ops:
  6.5 0.7 compare_select_fusion
  7.2 0.7 compare_and_fusion
  7.9 1.5 %copy.14 = bf16[1,1,2048,256]{2,3,1,0:T(8,128)(2,1)S(1)} copy(bf16[1,1,2048,256]{3,2,1,0:T(8,128)(2,1)} %param.3) | data formatting | bytes 2097152 | tf_op args[0]
  9.6 0.1 broadcast_multiply_fusion
  9.7 0.6 gather_fusion
  10.3 5.5 %fusion.30 = bf16[256,1,1,2048]{3,2,1,0:T(2,128)(2,1)} fusion(bf16[1,1,2048,256]{2,3,1,0:T(8,128)(2,1)S(1)} %bitcast.32, pred[256]{0:T(512)(128)(4,1)S(1)} %broadcast_in_dim.27), kind=kLoop, calls=%fused_computation.71 | loop fusion | flops 524288 | bytes 2097408
  15.8 0.5 broadcast.136
  16.3 8.0 %reduce.2 = bf16[256,2048]{1,0:T(8,128)(2,1)S(1)} reduce(bf16[256,1,1,2048]{3,2,1,0:T(2,128)(2,1)} %fusion.30, bf16[]{:T(256)} %broadcast.136), dimensions={1,2}, to_apply=%fusion.30.reduce_sub_computation | reduce | bytes 2097154
  24.3 2.0 %reshape.102 = bf16[4,2,65536]{2,1,0:T(2,128)(2,1)} reshape(bf16[256,2048]{1,0:T(8,128)(2,1)S(1)} %reduce.2) | data formatting | bytes 2097152
  26.4 5.4 %all-to-all-start = ((bf16[4,2,65536]{2,1,0:T(2,128)(2,1)}), bf16[4,2,65536]{2,1,0:T(2,128)(2,1)S(1)}, u32[]{:S(2)}, u32[]{:S(2)}) async-start(bf16[4,2,65536]{2,1,0:T(2,128)(2,1)} %reshape.102), calls=%async_computation | async-start | bytes 2097152 | tf_op jit(solution)/shard_map/all_to_all | solution.py:79
  31.8 36.4 %cosine_convert_fusion.1 = (bf16[2048,512]{1,0:T(8,128)(2,1)}, bf16[2048,512]{1,0:T(8,128)(2,1)}, bf16[2048,512]{1,0:T(8,128)(2,1)}, bf16[2048,512]{1,0:T(8,128)(2,1)}) fusion(s32[512]{0:T(512)S(1)} %iota_add_fusion.1, s32[2048]{0:T(1024)S(1)} %iota_add_fusion), kind=kLoop, calls=%fused_computation.28 | loop fusion | flops 35651584 | bytes 8398848 | tf_op jit(solution)/shard_map/convert.10
  68.3 1.0 reshape.103
  69.2 0.6 copy.19
  69.9 1.0 copy-done.2
  70.8 2.8 %fusion.17 = f32[4,64,1024]{2,1,0:T(8,128)S(1)} fusion(bf16[4,2048,64]{1,2,0:T(8,128)(2,1)S(1)} %bitcast.34, bf16[2048,512]{1,0:T(8,128)(2,1)S(1)} %copy-done.2, bf16[2048,512]{1,0:T(8,128)(2,1)} %get-tuple-element.14), kind=kOutput, calls=%fused_computation.32 | convolution fusion | flops 1082654720 | bytes 6291456 | tf_op jit(solution)/shard_map/gfnc,nk->gfck/dot_general | solution.py:80
  74.2 0.2 copy.17
  74.5 1.5 %collective-permute-start = (bf16[4,64,1024]{2,1,0:T(8,128)(2,1)S(1)}, bf16[4,64,1024]{2,1,0:T(8,128)(2,1)S(1)}, u32[]{:S(2)}, u32[]{:S(2)}) collective-permute-start(bf16[4,64,1024]{2,1,0:T(8,128)(2,1)S(1)} %multiply_convert_fusion), channel_id=1, source_target_pairs={{0,4},{4,8},{8,12},{12,0},{1,5},{5,9},{9,13},{13,1},{2,6},{6,10},{... | collective-permute-start | bytes 1572872 | tf_op jit(solution)/shard_map/ppermute | solution.py:13
  76.0 12.8 %collective-permute-done = bf16[4,64,1024]{2,1,0:T(8,128)(2,1)S(1)} collective-permute-done((bf16[4,64,1024]{2,1,0:T(8,128)(2,1)S(1)}, bf16[4,64,1024]{2,1,0:T(8,128)(2,1)S(1)}, u32[]{:S(2)}, u32[]{:S(2)}) %collective-permute-start) | collective-permute-done | bytes 524320 | tf_op jit(solution)/shard_map/ppermute | solution.py:13
  88.8 13.3 %collective-permute-done.1 = bf16[4,64,1024]{2,1,0:T(8,128)(2,1)S(1)} collective-permute-done((bf16[4,64,1024]{2,1,0:T(8,128)(2,1)S(1)}, bf16[4,64,1024]{2,1,0:T(8,128)(2,1)S(1)}, u32[]{:S(2)}, u32[]{:S(2)}) %collective-permute-start.1) | collective-permute-done | bytes 524320 | tf_op jit(solution)/shard_map/ppermute | solution.py:13
  102.1 0.4 fusion.19
  102.6 2.2 %fusion.6 = f32[2048,128]{1,0:T(8,128)} fusion(bf16[128,1024]{1,0:T(8,128)(2,1)S(1)} %bitcast.35, bf16[2048,512]{1,0:T(8,128)(2,1)S(1)} %copy-done.1, bf16[2048,512]{1,0:T(8,128)(2,1)S(1)} %copy-done), kind=kOutput, calls=%fused_computation.15 | convolution fusion | flops 545259520 | bytes 5505024 | tf_op jit(solution)/shard_map/dot_general | solution.py:97
  104.9 25.4 %reduce-scatter.2.cloned.1.call-done = f32[512,128]{1,0:T(8,128)} async-done(((f32[2048,128]{1,0:T(8,128)}), f32[512,128]{1,0:T(8,128)}) %reduce-scatter.2.cloned.1.call-update) | async-done | bytes 262160 | tf_op jit(solution)/shard_map/reduce_scatter | solution.py:96
  130.3 1.0 broadcast_multiply_fusion.1
  131.2 0.8 copy.18
  (27 shorter events, 0.8 us)
Async XLA Ops:
  6.5 2.8 %copy-start.3 = (s32[256]{0:T(256)S(1)}, s32[256]{0:T(256)}, u32[]{:S(2)}) copy-start(s32[256]{0:T(256)} %param.4) | copy-start | bytes 3076
  26.4 41.9 %all-to-all-start = ((bf16[4,2,65536]{2,1,0:T(2,128)(2,1)}), bf16[4,2,65536]{2,1,0:T(2,128)(2,1)S(1)}, u32[]{:S(2)}, u32[]{:S(2)}) async-start(bf16[4,2,65536]{2,1,0:T(2,128)(2,1)} %reshape.102), calls=%async_computation | async-start | bytes 2097152 | tf_op jit(solution)/shard_map/all_to_all | solution.py:79
  31.8 98.5 %reduce-scatter.2.cloned.1.call-start = ((), (), s32[]{:S(2)}) async-start(), calls=%async_computation.2 | async-start | bytes 1310720 | tf_op jit(solution)/shard_map/reduce_scatter | solution.py:96
  69.2 1.6 %copy-start.2 = (bf16[2048,512]{1,0:T(8,128)(2,1)S(1)}, bf16[2048,512]{1,0:T(8,128)(2,1)}, u32[]{:S(2)}) copy-start(bf16[2048,512]{1,0:T(8,128)(2,1)} %get-tuple-element.13) | copy-start | bytes 6291460
  74.4 28.2 %copy-start = (bf16[2048,512]{1,0:T(8,128)(2,1)S(1)}, bf16[2048,512]{1,0:T(8,128)(2,1)}, u32[]{:S(2)}) copy-start(bf16[2048,512]{1,0:T(8,128)(2,1)} %get-tuple-element.11) | copy-start | bytes 6291460
  74.4 28.2 %copy-start.1 = (bf16[2048,512]{1,0:T(8,128)(2,1)S(1)}, bf16[2048,512]{1,0:T(8,128)(2,1)}, u32[]{:S(2)}) copy-start(bf16[2048,512]{1,0:T(8,128)(2,1)} %get-tuple-element.12) | copy-start | bytes 6291460
  74.5 14.3 %collective-permute-start = (bf16[4,64,1024]{2,1,0:T(8,128)(2,1)S(1)}, bf16[4,64,1024]{2,1,0:T(8,128)(2,1)S(1)}, u32[]{:S(2)}, u32[]{:S(2)}) collective-permute-start(bf16[4,64,1024]{2,1,0:T(8,128)(2,1)S(1)} %multiply_convert_fusion), channel_id=1, source_target_pairs={{0,4},{4,8},{8,12},{12,0},{1,5},{5,9},{9,13},{13,1},{2,6},{6,10},{... | collective-permute-start | bytes 1572872 | tf_op jit(solution)/shard_map/ppermute | solution.py:13
  88.8 13.3 %collective-permute-start.1 = (bf16[4,64,1024]{2,1,0:T(8,128)(2,1)S(1)}, bf16[4,64,1024]{2,1,0:T(8,128)(2,1)S(1)}, u32[]{:S(2)}, u32[]{:S(2)}) collective-permute-start(bf16[4,64,1024]{2,1,0:T(8,128)(2,1)S(1)} %collective-permute-done), channel_id=1, source_target_pairs={{0,4},{4,8},{8,12},{12,0},{1,5},{5,9},{9,13},{13,1},{2,6},{6,10},{... | collective-permute-start | bytes 1572872 | tf_op jit(solution)/shard_map/ppermute | solution.py:13
Sparse Core Ops, SparseCore 0:
  105.0 25.2 reduce-scatter.1
where the time goes:
time: 140 us; the launch traced here: 139 us
  other arithmetic  53.3 us (38%)
  waiting for transfers between devices  51.5 us (37%)
  between operations  13.6 us (10%)
  local copies, waits for them, and re-layouts  8.49 us (6%)
  starting transfers between devices  6.94 us (5%)
  matrix products  5.08 us (4%)
    another operation x1, other arithmetic  36.4 us
    ppermute x2, waiting for transfers between devices, passed_along(): lax.ppermute(shard, axis, [(i, (i + by) % count) for i in range(count)])  26.1 us
    reduce_scatter x1, waiting for transfers between devices, body(): lax.psum_scatter(lax.dot_general(inverse, flat, (((1,), (1,)), ((), ())),...  25.4 us
    unnamed x2, other arithmetic  13.5 us
    unnamed x13, local copies, waits for them, and re-layouts  6.58 us
    all_to_all x1, starting transfers between devices, body(): lax.all_to_all(ordered, 'chan', split_axis=3, concat_axis=1, tiled=True)  5.42 us
    dot_general x1, matrix products, body(): jnp.einsum('gfnc,nk->gfck', regrouped, forward, preferred_element_type=jn...  2.84 us
  transfers between devices with their start and end apart: 4, of which 3 were waited for; matrix products, arithmetic and copies ran while one was open for 26% of the time, Pallas kernels for 0%

commit v1 on v0

v1 whole, which is shorter than its diff:
```python
import functools
import math

import jax
import jax.numpy as jnp
import ml_dtypes
import numpy as np
from jax import lax
from jax.experimental import pallas as pl
from jax.experimental.pallas import tpu as pltpu
from jax.sharding import PartitionSpec as P

BAND = 16
MESH = pl.DeviceIdType.MESH


def trig_tables(samples, chans, times, lags):
    half = samples // 2
    bins = half // (lags * chans)
    rows = np.arange(samples, dtype=np.int64)
    phase = (rows[:, None] * np.arange(half)[None, :]) % samples
    angle = phase.astype(np.float32) * np.float32(2.0 * math.pi / samples)
    cosine = np.cos(angle).astype(ml_dtypes.bfloat16)
    sine = (-np.sin(angle)).astype(ml_dtypes.bfloat16)
    both = np.stack([a.reshape(samples, lags, chans, bins) for a in (cosine, sine)])
    both = both.transpose(2, 3, 1, 0, 4).reshape(lags, chans, samples, 2 * bins)
    forward = np.ascontiguousarray(both.transpose(0, 1, 3, 2))
    inverse = both[:, :, (rows + half) % samples]
    inverse = inverse.reshape(lags, chans, times, lags, samples // (times * lags), 2 * bins)
    inverse = inverse.transpose(0, 1, 3, 2, 4, 5).reshape(lags, chans, samples, 2 * bins)
    return forward, np.ascontiguousarray(inverse)


def kernel(
    chans, times, lags, rounds, norm,
    map_ref, mask_ref, x_ref, forward_hbm, inverse_hbm, out_ref,
    forward, inverse, pick, ordered, spec_out, spec, cross_out, cross, partial, core_out, core_in,
    time_out, time_in,
    forward_sem, inverse_sem, spec_send, spec_recv, cross_send, cross_recv, core_send, core_recv,
    time_send, time_recv,
):
    me, core, group = lax.axis_index("chan"), lax.axis_index("lag"), lax.axis_index("tm")
    samples, width_all = x_ref.shape
    width = width_all // chans
    bins = forward.shape[1] // 2
    lag_rows = out_ref.shape[0]

    def around(index, by, count):
        return lax.rem(index + by + count, count)

    barrier = pltpu.get_barrier_semaphore()
    for axis, index, count in (("chan", me, chans), ("lag", core, lags), ("tm", group, times)):
        for by in range(1, count):
            pl.semaphore_signal(
                barrier, inc=1, device_id={axis: around(index, by, count)}, device_id_type=MESH
            )

    def load_forward(s):
        return pltpu.make_async_copy(
            forward_hbm.at[core, around(me, s, chans)], forward.at[s], forward_sem.at[s]
        )

    def load_inverse(s):
        return pltpu.make_async_copy(
            inverse_hbm.at[core, around(me, -s, chans)], inverse.at[s], inverse_sem.at[s]
        )

    def send_spec(s):
        return pltpu.make_async_remote_copy(
            src_ref=spec_out.at[s], dst_ref=spec.at[s],
            send_sem=spec_send.at[s], recv_sem=spec_recv.at[s],
            device_id={"chan": around(me, s, chans)}, device_id_type=MESH,
        )

    def send_cross(s):
        return pltpu.make_async_remote_copy(
            src_ref=cross_out.at[around(me, s, chans)], dst_ref=cross.at[s],
            send_sem=cross_send.at[s], recv_sem=cross_recv.at[s],
            device_id={"chan": around(me, s, chans)}, device_id_type=MESH,
        )

    def send_core(s):
        return pltpu.make_async_remote_copy(
            src_ref=core_out.at[s], dst_ref=core_in.at[s],
            send_sem=core_send.at[s], recv_sem=core_recv.at[s],
            device_id={"lag": around(core, s, lags)}, device_id_type=MESH,
        )

    def send_time(s):
        return pltpu.make_async_remote_copy(
            src_ref=time_out.at[s], dst_ref=time_in.at[s],
            send_sem=time_send.at[s], recv_sem=time_recv.at[s],
            device_id={"tm": around(group, s, times)}, device_id_type=MESH,
        )

    def each(low, high, work):
        def step(s, carry):
            work(s)
            return carry

        lax.fori_loop(low, high, step, 0)

    each(1, chans, lambda s: load_forward(s).start())
    load_forward(0).start()
    each(0, chans, lambda s: load_inverse(s).start())

    for p in range(chans):
        source = map_ref[p] * width + lax.broadcasted_iota(jnp.int32, (width, width_all), 0)
        channel = lax.broadcasted_iota(jnp.int32, (width, width_all), 1)
        kept = jnp.where(source == channel, mask_ref[...], 0)
        pick[p * width:(p + 1) * width, :] = kept.astype(jnp.float32).astype(jnp.bfloat16)
    tile = min(512, samples)

    def order(i):
        rows = pl.ds(pl.multiple_of(i * tile, tile), tile)
        ordered[rows, :] = lax.dot_general(
            x_ref[rows, :], pick[...], (((1,), (1,)), ((), ())),
            preferred_element_type=jnp.float32,
        ).astype(jnp.bfloat16)

    each(0, samples // tile, order)

    def transform(s):
        load_forward(s).wait()
        return jnp.dot(
            forward[s], ordered[...], preferred_element_type=jnp.float32
        ).astype(jnp.bfloat16)

    pl.semaphore_wait(barrier, chans + lags + times - 3)

    def transform_and_send(s):
        spec_out[s] = transform(s)
        send_spec(s).start()

    each(1, chans, transform_and_send)
    spec[0] = transform(0)
    each(1, chans, lambda s: send_spec(s).wait_recv())

    part = min(32, bins)
    freq_base = core * (bins * chans) + me * bins

    def cross_part(i):
        low = pl.multiple_of(i * part, part)
        re_rows = pl.ds(low, part)
        im_rows = pl.ds(pl.multiple_of(bins + i * part, part), part)
        power = jnp.zeros((part, width_all), jnp.float32)
        for f in range(chans):
            re = spec[f, re_rows, :].astype(jnp.float32)
            im = spec[f, im_rows, :].astype(jnp.float32)
            power = power + (re * re + im * im)
        banded = jnp.sum(power.reshape(part // BAND, BAND, width_all), axis=1, keepdims=True)
        scale = 1.0 / jnp.sqrt(banded / float(chans * BAND) + 1e-06)
        scale = jnp.broadcast_to(scale, (part // BAND, BAND, width_all)).reshape(part, width_all)
        freq = (freq_base + low + lax.broadcasted_iota(jnp.int32, (part, width_all), 0)).astype(
            jnp.float32
        )
        ramp_width = float(max(samples // 128, 1))
        lower = jnp.clip((freq - float(samples // 256)) / ramp_width, 0.0, 1.0)
        upper = jnp.clip((0.45 * samples - freq) / ramp_width, 0.0, 1.0)
        factor = scale * (lower * upper)
        re_sum = [jnp.zeros((part, width_all), jnp.float32) for _ in range(rounds)]
        im_sum = [jnp.zeros((part, width_all), jnp.float32) for _ in range(rounds)]
        for f in range(chans):
            re = (spec[f, re_rows, :].astype(jnp.float32) * factor).astype(jnp.bfloat16)
            im = (spec[f, im_rows, :].astype(jnp.float32) * factor).astype(jnp.bfloat16)
            re, im = re.astype(jnp.float32), im.astype(jnp.float32)
            for r in range(rounds):
                re_far = pltpu.roll(re, (r + 1) * width, 1)
                im_far = pltpu.roll(im, (r + 1) * width, 1)
                re_sum[r] = re_sum[r] + (re * re_far + im * im_far)
                im_sum[r] = im_sum[r] + (im * re_far - re * im_far)
        for c in range(chans):
            own = slice(c * width, (c + 1) * width)
            cross_out[c, re_rows, :] = jnp.concatenate(
                [a[:, own] for a in re_sum], axis=1
            ).astype(jnp.bfloat16)
            cross_out[c, im_rows, :] = jnp.concatenate(
                [a[:, own] for a in im_sum], axis=1
            ).astype(jnp.bfloat16)

    each(0, bins // part, cross_part)
    each(1, chans, lambda s: send_cross(s).start())
    cross[0] = cross_out[me]

    def invert(s):
        load_inverse(s).wait()
        return jnp.dot(inverse[s], cross[s], preferred_element_type=jnp.float32)

    partial[...] = invert(0)

    def invert_more(s):
        send_cross(s).wait_recv()
        partial[...] += invert(s)

    each(1, chans, invert_more)

    def rows_of(lag_block):
        count = times * lag_rows
        return pl.ds(pl.multiple_of(lag_block * count, count), count)

    for s in range(1, lags):
        core_out[s] = partial[rows_of(around(core, s, lags)), :].astype(jnp.bfloat16)
        send_core(s).start()
    total = partial[rows_of(core), :]
    for s in range(1, lags):
        send_core(s).wait_recv()
        total = total + core_in[s].astype(jnp.float32)
    partial[0:times * lag_rows, :] = total

    def own_lags(index):
        return partial[pl.ds(pl.multiple_of(index * lag_rows, lag_rows), lag_rows), :]

    for s in range(1, times):
        time_out[s] = own_lags(around(group, s, times)).astype(jnp.bfloat16)
        send_time(s).start()
    result = own_lags(group)
    for s in range(1, times):
        send_time(s).wait_recv()
        result = result + time_in[s].astype(jnp.float32)
    out_ref[...] = result * norm

    each(1, chans, lambda s: send_spec(s).wait_send())
    each(1, chans, lambda s: send_cross(s).wait_send())
    for s in range(1, lags):
        send_core(s).wait_send()
    for s in range(1, times):
        send_time(s).wait_send()


def body(forward_table, inverse_table, records, dead_mask, block_map):
    chans, lags, times = lax.axis_size("chan"), lax.axis_size("lag"), lax.axis_size("tm")
    samples, width_all = records.shape[2:]
    width = width_all // chans
    rounds = min(4, chans // 2)
    bins = samples // (2 * lags * chans)
    lag_rows = samples // (times * lags)
    columns = rounds * width
    norm = 1.0 / math.sqrt(samples // 2 * chans * times)
    vmem = pl.BlockSpec(memory_space=pltpu.VMEM)
    bf16, dma = jnp.bfloat16, pltpu.SemaphoreType.DMA
    stacked = pl.pallas_call(
        functools.partial(kernel, chans, times, lags, rounds, norm),
        out_shape=jax.ShapeDtypeStruct((lag_rows, columns), jnp.float32),
        in_specs=[
            pl.BlockSpec(memory_space=pltpu.SMEM), vmem, vmem,
            pl.BlockSpec(memory_space=pl.ANY), pl.BlockSpec(memory_space=pl.ANY),
        ],
        out_specs=vmem,
        scratch_shapes=[
            pltpu.VMEM((chans, 2 * bins, samples), bf16),
            pltpu.VMEM((chans, samples, 2 * bins), bf16),
            pltpu.VMEM((width_all, width_all), bf16),
            pltpu.VMEM((samples, width_all), bf16),
            pltpu.VMEM((chans, 2 * bins, width_all), bf16),
            pltpu.VMEM((chans, 2 * bins, width_all), bf16),
            pltpu.VMEM((chans, 2 * bins, columns), bf16),
            pltpu.VMEM((chans, 2 * bins, columns), bf16),
            pltpu.VMEM((samples, columns), jnp.float32),
            pltpu.VMEM((lags, times * lag_rows, columns), bf16),
            pltpu.VMEM((lags, times * lag_rows, columns), bf16),
            pltpu.VMEM((times, lag_rows, columns), bf16),
            pltpu.VMEM((times, lag_rows, columns), bf16),
            dma((chans,)), dma((chans,)), dma((chans,)), dma((chans,)), dma((chans,)), dma((chans,)),
            dma((lags,)), dma((lags,)), dma((times,)), dma((times,)),
        ],
        compiler_params=pltpu.CompilerParams(
            collective_id=0, has_side_effects=True, vmem_limit_bytes=58 * 1024 * 1024
        ),
    )(block_map, dead_mask.reshape(1, width_all), records[0, 0], forward_table, inverse_table)
    return stacked.reshape(lag_rows, rounds, width)


def solution(mesh):
    shape = mesh.shape

    def run(records, dead_mask, block_map):
        tables = trig_tables(records.shape[2], shape["chan"], shape["tm"], shape["lag"])
        forward_table, inverse_table = (jnp.asarray(a) for a in tables)
        return jax.shard_map(
            body,
            mesh=mesh,
            in_specs=(P(), P(), P(("grp", "tm"), "chan", None, None), P("grp"), P("grp")),
            out_specs=P(("grp", "tm", "lag"), None, "chan"),
            check_vma=False,
        )(forward_table, inverse_table, records, dead_mask, block_map)

    return run
```

time: 140 us -> 34.9 us (0.25)
  other arithmetic: 53.3 us -> 0 us
  waiting for transfers between devices: 51.5 us -> 0 us
  Pallas kernels: 0 us -> 33 us
  between operations: 13.6 us -> 0.01 us
  starting transfers between devices: 6.94 us -> 0 us
  local copies, waits for them, and re-layouts: 8.49 us -> 1.79 us
  matrix products: 5.08 us -> 0 us
    another operation x3 -> x0, other arithmetic: 36.5 us -> none
    pallas_call x0 -> x1, Pallas kernels: none -> 33 us  [body(): pl.pallas_call(functools.partial(kernel, chans, times, lags, rounds, norm...]
    ppermute x2 -> x0, waiting for transfers between devices: 26.1 us -> none  [passed_along(): lax.ppermute(shard, axis, [(i, (i + by) % count) for i in range(count)])]
    reduce_scatter x1 -> x0, waiting for transfers between devices: 25.4 us -> none  [body(): lax.psum_scatter(lax.dot_general(inverse, flat, (((1,), (1,)), ((), ())),...]
    unnamed x2 -> x0, other arithmetic: 13.5 us -> none
    unnamed x13 -> x0, local copies, waits for them, and re-layouts: 6.58 us -> none
    all_to_all x1 -> x0, starting transfers between devices: 5.42 us -> none  [body(): lax.all_to_all(ordered, 'chan', split_axis=3, concat_axis=1, tiled=True)]
    dot_general x2 -> x0, matrix products: 5.08 us -> none  [the longest x1 2.84 us: body(): jnp.einsum('gfnc,nk->gfck', regrouped, forward, preferred_element_type=jn...]
  transfers between devices with their start and end apart: 4 -> 0, of which waited for: 3 -> 0; matrix products, arithmetic and copies ran while one was open for 26% -> 0% of each run, Pallas kernels for 0% -> 0%
where the time goes in v1:
time: 34.9 us; the launch traced here: 34.8 us
  Pallas kernels  33 us (95%)
  local copies, waits for them, and re-layouts  1.79 us (5%)
    pallas_call x1, Pallas kernels, body(): pl.pallas_call(functools.partial(kernel, chans, times, lags, rounds, norm...  33 us
    pallas_call x1, local copies, waits for them, and re-layouts, body(): pl.pallas_call(functools.partial(kernel, chans, times, lags, rounds, norm...  1.79 us

profile of v1, /device:TPU:1, one launch (start us, length us, event | category | flops | bytes accessed | tf_op | source)
XLA Modules:
  0.0 34.8 jit_solution(18250185983030170043)
XLA Ops:
  0.0 33.0 %shard_map.55 = f32[512,128]{1,0:T(8,128)} custom-call(s32[4]{0:T(128)} %map_ref.1, s32[1,256]{1,0:T(1,128)} %bitcast.4, bf16[2048,256]{1,0:T(8,128)(2,1)} %bitcast.3, bf16[2,4,256,2048]{3,2,1,0:T(8,128)(2,1)} %constant.4.clone.forward_hbm, bf16[2,4,2048,256]{3,2,1,0:T(8,128)(2,1)} %constant.5.clone.inverse_hbm), custom_call_target="tpu_custom_call" | custom-call | tf_op jit(solution)/shard_map/pallas_call | solution.py:241
  33.0 1.8 %copy.7 = f32[512,128]{0,1:T(8,128)} copy(f32[512,128]{1,0:T(8,128)} %shard_map.55) | data formatting | bytes 524288 | tf_op jit(solution)/shard_map/pallas_call | solution.py:241

commit v2 on v1

v2 whole, which is shorter than its diff:
```python
import functools
import math

import jax
import jax.numpy as jnp
import ml_dtypes
import numpy as np
from jax import lax
from jax.experimental import pallas as pl
from jax.experimental.pallas import tpu as pltpu
from jax.sharding import PartitionSpec as P

BAND = 16
HALVES = 2
MESH = pl.DeviceIdType.MESH


def trig_tables(samples, chans, times, lags, halves):
    half = samples // 2
    bins = half // (lags * chans * halves)
    rows = np.arange(samples, dtype=np.int64)
    phase = (np.arange(half)[:, None] * rows[None, :]) % samples
    angle = phase.astype(np.float32) * np.float32(2.0 * math.pi / samples)
    cosine = np.cos(angle).astype(ml_dtypes.bfloat16)
    sine = (-np.sin(angle)).astype(ml_dtypes.bfloat16)
    both = np.stack([a.reshape(lags, chans, halves, bins, samples) for a in (cosine, sine)], axis=3)
    forward = both.reshape(lags, chans, halves, 2 * bins, samples)
    inverse = both.reshape(lags, chans, 2 * halves * bins, samples)[..., (rows + half) % samples]
    inverse = inverse.reshape(inverse.shape[:3] + (times * lags, samples // (times * lags)))
    return forward, np.ascontiguousarray(inverse.transpose(3, 0, 1, 2, 4))


def kernel(
    chans, times, lags, rounds, halves, norm,
    map_ref, mask_ref, x_ref, forward_hbm, inverse_hbm, out_ref,
    forward, inverse, pick, ordered, spec_out, spec, cross_out, cross, far, summed,
    forward_sem, inverse_sem, spec_send, spec_recv, cross_send, cross_recv, far_send, far_recv,
    core_send, core_recv,
):
    me, core, group = lax.axis_index("chan"), lax.axis_index("lag"), lax.axis_index("tm")
    samples, width_all = x_ref.shape
    width = width_all // chans
    bins = forward.shape[2] // 2
    columns, lag_rows = out_ref.shape

    def around(index, by, count):
        return lax.rem(index + by + count, count)

    barrier = pltpu.get_barrier_semaphore()
    for axis, index, count in (("chan", me, chans), ("lag", core, lags), ("tm", group, times)):
        for by in range(1, count):
            pl.semaphore_signal(
                barrier, inc=1, device_id={axis: around(index, by, count)}, device_id_type=MESH
            )

    def load_forward(s, h):
        return pltpu.make_async_copy(
            forward_hbm.at[core, around(me, s, chans), h], forward.at[s, h], forward_sem.at[s, h]
        )

    def load_inverse(v, s):
        return pltpu.make_async_copy(
            inverse_hbm.at[group * lags + core, around(core, -v, lags), around(me, -s, chans)],
            inverse.at[v, s], inverse_sem.at[v, s],
        )

    def send_spec(s, h):
        return pltpu.make_async_remote_copy(
            src_ref=spec_out.at[s, h], dst_ref=spec.at[s, h],
            send_sem=spec_send.at[s, h], recv_sem=spec_recv.at[s, h],
            device_id={"chan": around(me, s, chans)}, device_id_type=MESH,
        )

    def send_cross(s, h):
        return pltpu.make_async_remote_copy(
            src_ref=cross_out.at[around(me, s, chans), h], dst_ref=cross.at[s, h],
            send_sem=cross_send.at[s, h], recv_sem=cross_recv.at[s, h],
            device_id={"chan": around(me, s, chans)}, device_id_type=MESH,
        )

    def send_far(u, s, h):
        return pltpu.make_async_remote_copy(
            src_ref=cross.at[s, h], dst_ref=far.at[u, s, h],
            send_sem=far_send.at[u, s, h], recv_sem=far_recv.at[u, s, h],
            device_id={"tm": around(group, u, times)}, device_id_type=MESH,
        )

    def send_core(v, s, h):
        return pltpu.make_async_remote_copy(
            src_ref=summed.at[0, s, h], dst_ref=summed.at[v, s, h],
            send_sem=core_send.at[v, s, h], recv_sem=core_recv.at[v, s, h],
            device_id={"lag": around(core, v, lags)}, device_id_type=MESH,
        )

    def each(low, high, work):
        def step(s, carry):
            work(s)
            return carry

        lax.fori_loop(low, high, step, 0)

    for h in range(halves):
        each(1, chans, lambda s: load_forward(s, h).start())
    for h in range(halves):
        load_forward(0, h).start()
    for v in range(lags):
        each(0, chans, lambda s: load_inverse(v, s).start())

    for p in range(chans):
        source = map_ref[p] * width + lax.broadcasted_iota(jnp.int32, (width, width_all), 0)
        channel = lax.broadcasted_iota(jnp.int32, (width, width_all), 1)
        kept = jnp.where(source == channel, mask_ref[...], 0)
        pick[p * width:(p + 1) * width, :] = kept.astype(jnp.float32).astype(jnp.bfloat16)
    tile = min(512, samples)

    def order(i):
        rows = pl.ds(pl.multiple_of(i * tile, tile), tile)
        ordered[rows, :] = lax.dot_general(
            x_ref[rows, :], pick[...], (((1,), (1,)), ((), ())),
            preferred_element_type=jnp.float32,
        ).astype(jnp.bfloat16)

    each(0, samples // tile, order)

    def transform(s, h):
        load_forward(s, h).wait()
        return jnp.dot(
            forward[s, h], ordered[...], preferred_element_type=jnp.float32
        ).astype(jnp.bfloat16)

    pl.semaphore_wait(barrier, chans + lags + times - 3)

    for h in range(halves):
        def transform_and_send(s):
            spec_out[s, h] = transform(s, h)
            send_spec(s, h).start()

        each(1, chans, transform_and_send)
    for h in range(halves):
        spec[0, h] = transform(0, h)

    part = min(32, bins)

    def cross_part(h, i):
        low = pl.multiple_of(i * part, part)
        re_rows = pl.ds(low, part)
        im_rows = pl.ds(pl.multiple_of(bins + i * part, part), part)
        power = jnp.zeros((part, width_all), jnp.float32)
        for f in range(chans):
            re = spec[f, h, re_rows, :].astype(jnp.float32)
            im = spec[f, h, im_rows, :].astype(jnp.float32)
            power = power + (re * re + im * im)
        banded = jnp.sum(power.reshape(part // BAND, BAND, width_all), axis=1, keepdims=True)
        scale = 1.0 / jnp.sqrt(banded / float(chans * BAND) + 1e-06)
        scale = jnp.broadcast_to(scale, (part // BAND, BAND, width_all)).reshape(part, width_all)
        freq_base = ((core * chans + me) * halves + h) * bins + low
        freq = (freq_base + lax.broadcasted_iota(jnp.int32, (part, width_all), 0)).astype(
            jnp.float32
        )
        ramp_width = float(max(samples // 128, 1))
        lower = jnp.clip((freq - float(samples // 256)) / ramp_width, 0.0, 1.0)
        upper = jnp.clip((0.45 * samples - freq) / ramp_width, 0.0, 1.0)
        factor = scale * (lower * upper)
        re_sum = [jnp.zeros((part, width_all), jnp.float32) for _ in range(rounds)]
        im_sum = [jnp.zeros((part, width_all), jnp.float32) for _ in range(rounds)]
        for f in range(chans):
            re = (spec[f, h, re_rows, :].astype(jnp.float32) * factor).astype(jnp.bfloat16)
            im = (spec[f, h, im_rows, :].astype(jnp.float32) * factor).astype(jnp.bfloat16)
            re, im = re.astype(jnp.float32), im.astype(jnp.float32)
            for r in range(rounds):
                re_far = pltpu.roll(re, (r + 1) * width, 1)
                im_far = pltpu.roll(im, (r + 1) * width, 1)
                re_sum[r] = re_sum[r] + (re * re_far + im * im_far)
                im_sum[r] = im_sum[r] + (im * re_far - re * im_far)
        for c in range(chans):
            own = slice(c * width, (c + 1) * width)
            cross_out[c, h, re_rows, :] = jnp.concatenate(
                [a[:, own] for a in re_sum], axis=1
            ).astype(jnp.bfloat16)
            cross_out[c, h, im_rows, :] = jnp.concatenate(
                [a[:, own] for a in im_sum], axis=1
            ).astype(jnp.bfloat16)

    def start_far(s, h):
        for u in range(1, times):
            send_far(u, s, h).start()

    def sum_groups(s, h):
        total = cross[s, h].astype(jnp.float32)
        for u in range(1, times):
            send_far(u, s, h).wait_recv()
            total = total + far[u, s, h].astype(jnp.float32)
        summed[0, s, h] = total.astype(jnp.bfloat16)
        for v in range(1, lags):
            send_core(v, s, h).start()

    def pass_on(s, h):
        send_cross(s, h).wait_recv()
        start_far(s, h)

    for h in range(halves):
        each(1, chans, lambda s: send_spec(s, h).wait_recv())
        each(0, bins // part, lambda i: cross_part(h, i))
        each(1, chans, lambda s: send_cross(s, h).start())
        cross[0, h] = cross_out[me, h]
        start_far(0, h)
    for h in range(halves):
        each(1, chans, lambda s: pass_on(s, h))
        each(0, chans, lambda s: sum_groups(s, h))

    def invert(v):
        each(0, chans, lambda s: load_inverse(v, s).wait())
        depth = chans * halves * 2 * bins
        return lax.dot_general(
            summed[v].reshape(depth, columns), inverse[v].reshape(depth, lag_rows),
            (((0,), (0,)), ((), ())), preferred_element_type=jnp.float32,
        )

    result = invert(0)
    for v in range(1, lags):
        for h in range(halves):
            each(0, chans, lambda s: send_core(v, s, h).wait_recv())
        result = result + invert(v)
    out_ref[...] = result * norm

    for h in range(halves):
        each(1, chans, lambda s: send_spec(s, h).wait_send())
        each(1, chans, lambda s: send_cross(s, h).wait_send())
        for u in range(1, times):
            each(0, chans, lambda s: send_far(u, s, h).wait_send())
        for v in range(1, lags):
            each(0, chans, lambda s: send_core(v, s, h).wait_send())


def body(forward_table, inverse_table, records, dead_mask, block_map):
    chans, lags, times = lax.axis_size("chan"), lax.axis_size("lag"), lax.axis_size("tm")
    samples, width_all = records.shape[2:]
    width = width_all // chans
    rounds = min(4, chans // 2)
    halves = HALVES
    bins = samples // (2 * lags * chans * halves)
    lag_rows = samples // (times * lags)
    columns = rounds * width
    norm = 1.0 / math.sqrt(samples // 2 * chans * times)
    vmem = pl.BlockSpec(memory_space=pltpu.VMEM)
    bf16, dma = jnp.bfloat16, pltpu.SemaphoreType.DMA
    piece = (chans, halves, 2 * bins)
    stacked = pl.pallas_call(
        functools.partial(kernel, chans, times, lags, rounds, halves, norm),
        out_shape=jax.ShapeDtypeStruct((columns, lag_rows), jnp.float32),
        in_specs=[
            pl.BlockSpec(memory_space=pltpu.SMEM), vmem, vmem,
            pl.BlockSpec(memory_space=pl.ANY), pl.BlockSpec(memory_space=pl.ANY),
        ],
        out_specs=vmem,
        scratch_shapes=[
            pltpu.VMEM(piece + (samples,), bf16),
            pltpu.VMEM((lags, chans, 2 * halves * bins, lag_rows), bf16),
            pltpu.VMEM((width_all, width_all), bf16),
            pltpu.VMEM((samples, width_all), bf16),
            pltpu.VMEM(piece + (width_all,), bf16),
            pltpu.VMEM(piece + (width_all,), bf16),
            pltpu.VMEM(piece + (columns,), bf16),
            pltpu.VMEM(piece + (columns,), bf16),
            pltpu.VMEM((times,) + piece + (columns,), bf16),
            pltpu.VMEM((lags,) + piece + (columns,), bf16),
            dma((chans, halves)), dma((lags, chans)),
            dma((chans, halves)), dma((chans, halves)), dma((chans, halves)), dma((chans, halves)),
            dma((times, chans, halves)), dma((times, chans, halves)),
            dma((lags, chans, halves)), dma((lags, chans, halves)),
        ],
        compiler_params=pltpu.CompilerParams(
            collective_id=0, has_side_effects=True, vmem_limit_bytes=58 * 1024 * 1024
        ),
    )(block_map, dead_mask.reshape(1, width_all), records[0, 0], forward_table, inverse_table)
    return stacked.reshape(rounds, width, lag_rows).transpose(2, 0, 1)


def solution(mesh):
    shape = mesh.shape

    def run(records, dead_mask, block_map):
        tables = trig_tables(records.shape[2], shape["chan"], shape["tm"], shape["lag"], HALVES)
        forward_table, inverse_table = (jnp.asarray(a) for a in tables)
        return jax.shard_map(
            body,
            mesh=mesh,
            in_specs=(P(), P(), P(("grp", "tm"), "chan", None, None), P("grp"), P("grp")),
            out_specs=P(("grp", "tm", "lag"), None, "chan"),
            check_vma=False,
        )(forward_table, inverse_table, records, dead_mask, block_map)

    return run
```

time: 34.9 us -> 35.6 us (1.020)
  Pallas kernels: 33 us -> 33.7 us
    pallas_call x1 -> x0, local copies, waits for them, and re-layouts: 1.79 us -> none  [body(): pl.pallas_call(functools.partial(kernel, chans, times, lags, rounds, norm...]
    unnamed x0 -> x1, local copies, waits for them, and re-layouts: none -> 1.67 us
    pallas_call x1, Pallas kernels: 33 us -> 33.7 us  [body(): pl.pallas_call(functools.partial(kernel, chans, times, lags, rounds, halv...]
where the time goes in v2:
time: 35.6 us; the launch traced here: 35.4 us
  Pallas kernels  33.7 us (95%)
  local copies, waits for them, and re-layouts  1.67 us (5%)
    pallas_call x1, Pallas kernels, body(): pl.pallas_call(functools.partial(kernel, chans, times, lags, rounds, halv...  33.7 us
    unnamed x1, local copies, waits for them, and re-layouts  1.67 us

profile of v2, /device:TPU:1, one launch (start us, length us, event | category | flops | bytes accessed | tf_op | source)
XLA Modules:
  0.0 35.4 jit_solution(3386363021116945000)
XLA Ops:
  0.0 33.7 %shard_map.55 = f32[128,512]{1,0:T(8,128)} custom-call(s32[4]{0:T(128)} %map_ref.1, s32[1,256]{1,0:T(1,128)} %bitcast.7, bf16[2048,256]{1,0:T(8,128)(2,1)} %bitcast.6, bf16[2,4,2,128,2048]{4,3,2,1,0:T(8,128)(2,1)} %constant.4.clone.forward_hbm, bf16[4,2,4,256,512]{4,3,2,1,0:T(8,128)(2,1)} %constant.5.clone.inverse_hbm), custom_call_target="tpu_custom_call" | custom-call | tf_op jit(solution)/shard_map/pallas_call | solution.py:248
  33.7 1.7 %copy.7 = f32[512,2,64]{0,2,1:T(8,128)} copy(f32[512,2,64]{0,2,1:T(8,128)} %bitcast.5) | data formatting | bytes 524288

commit v3 on v2

--- a/solution.py
+++ b/solution.py
@@ -11,7 +11,7 @@
 from jax.sharding import PartitionSpec as P
 
 BAND = 16
-HALVES = 2
+HALVES = 1
 MESH = pl.DeviceIdType.MESH
 
 
@@ -53,6 +53,8 @@
                 barrier, inc=1, device_id={axis: around(index, by, count)}, device_id_type=MESH
             )
 
+    by_reach = sorted(range(1, chans), key=lambda s: abs(s - chans // 2))
+
     def load_forward(s, h):
         return pltpu.make_async_copy(
             forward_hbm.at[core, around(me, s, chans), h], forward.at[s, h], forward_sem.at[s, h]
@@ -128,16 +130,20 @@
             forward[s, h], ordered[...], preferred_element_type=jnp.float32
         ).astype(jnp.bfloat16)
 
+    for h in range(halves):
+        def transform_out(s):
+            spec_out[s, h] = transform(s, h)
+
+        each(1, chans, transform_out)
     pl.semaphore_wait(barrier, chans + lags + times - 3)
-
-    for h in range(halves):
-        def transform_and_send(s):
-            spec_out[s, h] = transform(s, h)
-            send_spec(s, h).start()
-
-        each(1, chans, transform_and_send)
+    for s in by_reach:
+        send_spec(s, 0).start()
     for h in range(halves):
         spec[0, h] = transform(0, h)
+
+    def send_next(s, h):
+        send_spec(s, h).wait_send()
+        send_spec(s, h + 1).start()
 
     part = min(32, bins)
 
@@ -199,14 +205,17 @@
         start_far(s, h)
 
     for h in range(halves):
+        if h + 1 < halves:
+            each(1, chans, lambda s: send_next(s, h))
         each(1, chans, lambda s: send_spec(s, h).wait_recv())
         each(0, bins // part, lambda i: cross_part(h, i))
         each(1, chans, lambda s: send_cross(s, h).start())
         cross[0, h] = cross_out[me, h]
         start_far(0, h)
-    for h in range(halves):
+        if h > 0:
+            each(0, chans, lambda s: sum_groups(s, h - 1))
         each(1, chans, lambda s: pass_on(s, h))
-        each(0, chans, lambda s: sum_groups(s, h))
+    each(0, chans, lambda s: sum_groups(s, halves - 1))
 
     def invert(v):
         each(0, chans, lambda s: load_inverse(v, s).wait())
@@ -224,7 +233,8 @@
     out_ref[...] = result * norm
 
     for h in range(halves):
-        each(1, chans, lambda s: send_spec(s, h).wait_send())
+        if h + 1 == halves:
+            each(1, chans, lambda s: send_spec(s, h).wait_send())
         each(1, chans, lambda s: send_cross(s, h).wait_send())
         for u in range(1, times):
             each(0, chans, lambda s: send_far(u, s, h).wait_send())

time: 35.6 us -> 34.2 us (0.961)
  Pallas kernels: 33.7 us -> 32.3 us
    pallas_call x1, Pallas kernels: 33.7 us -> 32.3 us  [body(): pl.pallas_call(functools.partial(kernel, chans, times, lags, rounds, halv...]
where the time goes in v3:
time: 34.2 us; the launch traced here: 34 us
  Pallas kernels  32.3 us (94%)
  local copies, waits for them, and re-layouts  1.67 us (5%)
    pallas_call x1, Pallas kernels, body(): pl.pallas_call(functools.partial(kernel, chans, times, lags, rounds, halv...  32.3 us
    unnamed x1, local copies, waits for them, and re-layouts  1.67 us

profile of v3, /device:TPU:1, one launch (start us, length us, event | category | flops | bytes accessed | tf_op | source)
XLA Modules:
  0.0 34.0 jit_solution(13851087570750528233)
XLA Ops:
  0.0 32.3 %shard_map.55 = f32[128,512]{1,0:T(8,128)} custom-call(s32[4]{0:T(128)} %map_ref.1, s32[1,256]{1,0:T(1,128)} %bitcast.7, bf16[2048,256]{1,0:T(8,128)(2,1)} %bitcast.6, bf16[2,4,1,256,2048]{4,3,2,1,0:T(8,128)(2,1)} %constant.4.clone.forward_hbm, bf16[4,2,4,256,512]{4,3,2,1,0:T(8,128)(2,1)} %constant.5.clone.inverse_hbm), custom_call_target="tpu_custom_call" | custom-call | tf_op jit(solution)/shard_map/pallas_call | solution.py:258
  32.3 1.7 %copy.7 = f32[512,2,64]{0,2,1:T(8,128)} copy(f32[512,2,64]{0,2,1:T(8,128)} %bitcast.5) | data formatting | bytes 524288

commit v4 on v3

--- a/solution.py
+++ b/solution.py
@@ -227,9 +227,14 @@
 
     result = invert(0)
     for v in range(1, lags):
-        for h in range(halves):
-            each(0, chans, lambda s: send_core(v, s, h).wait_recv())
-        result = result + invert(v)
+        each(0, chans, lambda s: load_inverse(v, s).wait())
+        for s in range(chans):
+            for h in range(halves):
+                send_core(v, s, h).wait_recv()
+            result = result + lax.dot_general(
+                summed[v, s].reshape(halves * 2 * bins, columns), inverse[v, s],
+                (((0,), (0,)), ((), ())), preferred_element_type=jnp.float32,
+            )
     out_ref[...] = result * norm
 
     for h in range(halves):

time: 34.2 us -> 33.7 us (0.985)
  Pallas kernels: 32.3 us -> 31.9 us
    pallas_call x1, Pallas kernels: 32.3 us -> 31.9 us  [body(): pl.pallas_call(functools.partial(kernel, chans, times, lags, rounds, halv...]
where the time goes in v4:
time: 33.7 us; the launch traced here: 33.5 us
  Pallas kernels  31.9 us (95%)
  local copies, waits for them, and re-layouts  1.67 us (5%)
    pallas_call x1, Pallas kernels, body(): pl.pallas_call(functools.partial(kernel, chans, times, lags, rounds, halv...  31.9 us
    unnamed x1, local copies, waits for them, and re-layouts  1.67 us

profile of v4, /device:TPU:1, one launch (start us, length us, event | category | flops | bytes accessed | tf_op | source)
XLA Modules:
  0.0 33.5 jit_solution(10802823427991407003)
XLA Ops:
  0.0 31.9 %shard_map.55 = f32[128,512]{1,0:T(8,128)} custom-call(s32[4]{0:T(128)} %map_ref.1, s32[1,256]{1,0:T(1,128)} %bitcast.7, bf16[2048,256]{1,0:T(8,128)(2,1)} %bitcast.6, bf16[2,4,1,256,2048]{4,3,2,1,0:T(8,128)(2,1)} %constant.4.clone.forward_hbm, bf16[4,2,4,256,512]{4,3,2,1,0:T(8,128)(2,1)} %constant.5.clone.inverse_hbm), custom_call_target="tpu_custom_call" | custom-call | tf_op jit(solution)/shard_map/pallas_call | solution.py:263
  31.9 1.7 %copy.7 = f32[512,2,64]{0,2,1:T(8,128)} copy(f32[512,2,64]{0,2,1:T(8,128)} %bitcast.5) | data formatting | bytes 524288
